TPU v7x, 256 devices: a whole 4x4x8 slice. The times are simulated.
256 devices in a mesh: row: 4 (over z_hi, core), col: 16 (over z_lo, x), depth: 4 (over y).
Axes of the slice: x: 4, y: 4, z: 8 (z_hi: 2, z_lo: 4; z = z_hi * 4 + z_lo), core: 2. Of those that a mesh axis runs over, the one named last changes fastest.
Arguments:
- tokens: bfloat16 [1536, 6144], P(('depth', 'col'), 'row'), may hold values from -6 to 6
- w_in: bfloat16 [6144, 24576], P('row', 'col'), may hold values from -0.078125 to 0.078125
- w_out: bfloat16 [24576, 6144], P('col', 'row'), may hold values from -0.0390625 to 0.0390625
- grad_out: bfloat16 [1536, 6144], P(('depth', 'col'), 'row'), may hold values from -6 to 6
Outputs:
- layer_out: bfloat16 [1536, 6144], P(('depth', 'col'), 'row')
- grad_tokens: bfloat16 [1536, 6144], P(('depth', 'col'), 'row')
- grad_w_in: bfloat16 [6144, 24576], P(('row', 'depth'), 'col')
- grad_w_out: bfloat16 [24576, 6144], P(('col', 'depth'), 'row')
All inputs are finite; a program needn't handle non-finite values.
Results may differ from a plain program's by a relative error of at most 0.0049.
Values may be sent and summed in bfloat16 or wider, within the bound.
No kernel may reach another device: no remote copies, remote signals or barrier semaphores. Data moves between devices by JAX's collectives and lax.ppermute only.
A program may use at most 128 MiB of HBM per device.

v0:
```python
import jax
import jax.numpy as jnp
from jax import lax
from jax.sharding import PartitionSpec as P

coef = 0.7978845608
AXES = ("row", "col", "depth")
BF = jnp.bfloat16
F32 = jnp.float32


def gelu_pair(z):
    t = jnp.tanh(coef * (z + 0.044715 * z * z * z))
    value = 0.5 * z * (1.0 + t)
    slope = 0.5 * (1.0 + t) + 0.5 * z * (1.0 - t * t) * coef * (1.0 + 0.134145 * z * z)
    return (value, slope)


def dot(left, right, dims):
    return lax.dot_general(left, right, ((dims[:1], dims[1:]), ((), ())), preferred_element_type=F32)


def send(array, hi=0, core=0, lo=0, x=0, y=0):
    pairs = []
    for z_hi in range(2):
        for c in range(2):
            for z_lo in range(4):
                for i in range(4):
                    for j in range(4):
                        here = ((z_hi * 2 + c) * 16 + z_lo * 4 + i) * 4 + j
                        there = (
                            ((z_hi + hi) % 2 * 2 + (c + core) % 2) * 16 + (z_lo + lo) % 4 * 4 + (i + x) % 4
                        ) * 4 + (j + y) % 4
                        pairs.append((here, there))
    return lax.ppermute(array, AXES, pairs)


def exchange(array, turn):
    pairs = []
    for row in range(4):
        flip = 1 if row % 2 == turn else 3
        for col in range(16):
            for y in range(4):
                pairs.append(((row * 16 + col) * 4 + y, (row * 16 + col) * 4 + (y ^ flip)))
    return lax.ppermute(array, AXES, pairs)


def after(array, *others):
    return lax.optimization_barrier((array, *others))[0]


def front(token_block, cot_block, weights):
    in_mine, in_other, out_mine, out_other = weights
    other = jnp.stack([dot(token_block, in_other, (1, 0)).astype(BF), dot(cot_block, out_other, (1, 1)).astype(BF)])
    mine = jnp.stack([dot(token_block, in_mine, (1, 0)), dot(cot_block, out_mine, (1, 1))])
    return mine + send(other, core=1).astype(F32)


def cross(total):
    payload = total.astype(BF)
    return payload, send(payload, hi=1)


def middle(total, arrived):
    both = total + arrived.astype(F32)
    value, slope = gelu_pair(both[0])
    return jnp.stack([value.astype(BF), (both[1] * slope).astype(BF)])


def back(mine, other, weights):
    in_mine, in_other, out_mine, out_other = weights
    return jnp.stack(
        [
            dot(mine[0], out_mine, (1, 0)) + dot(other[0], out_other, (1, 0)),
            dot(mine[1], in_mine, (1, 1)) + dot(other[1], in_other, (1, 1)),
        ]
    )


def local(tokens, w_in, w_out, grad_out):
    core = lax.axis_index("row") % 2
    y = lax.axis_index("depth")
    weights = lax.optimization_barrier(
        (
            lax.dynamic_slice_in_dim(w_in, core * 768, 768, axis=1),
            lax.dynamic_slice_in_dim(w_in, (1 - core) * 768, 768, axis=1),
            lax.dynamic_slice_in_dim(w_out, core * 768, 768, axis=0),
            lax.dynamic_slice_in_dim(w_out, (1 - core) * 768, 768, axis=0),
        )
    )
    first = y ^ (1 + 2 * core)
    second = y ^ (3 - 2 * core)

    own = jnp.stack([tokens, grad_out])
    block0 = jnp.concatenate([own] + [send(own, lo=-k) for k in (1, 2, 3)], axis=1)
    block1 = send(block0, x=-1)
    block3 = send(block0, x=-3)
    near = jnp.concatenate([block1, block3], axis=1)
    total0 = front(block0[0], block0[1], weights)
    payload0, arrived0 = cross(total0)
    total1 = front(near[0], near[1], weights)
    payload1, arrived1 = cross(total1)
    block1, block3 = after(block1, payload1), after(block3, payload1)
    block2 = jnp.stack([send(block1[0], x=-1), send(block3[1], x=1)])
    total2 = front(block2[0], block2[1], weights)
    payload2, arrived2 = cross(total2)

    def split(rows, shift):
        def quarter(q):
            return lax.dynamic_slice_in_dim(rows, (q + shift) % 4 * 384, 384, axis=1)

        return quarter(y), quarter(second), jnp.concatenate([quarter(first), quarter(y ^ 2)], axis=1)

    def pair_rows(mine, other):
        own, second_part, out = split(jnp.concatenate([mine[0], other[0]], axis=1), 2 * core)
        low = jnp.where(core == 0, mine[1], other[1])
        high = jnp.where(core == 0, other[1], mine[1])
        grad = jnp.concatenate([low, high], axis=1)
        return own, second_part, grad, jnp.concatenate([out, grad], axis=1)

    token0 = split(jnp.concatenate([block0[0], near[0]], axis=0), 0)
    cot0 = jnp.concatenate([block0[1], near[1]], axis=0)
    far0 = exchange(after(jnp.concatenate([cot0, token0[2]], axis=1), payload1), 0)
    token1 = split(block2[0], 0)

    mine0 = middle(total0, after(arrived0, payload2))
    other0 = send(mine0, core=1)
    pair0 = pair_rows(mine0, other0)
    far1 = exchange(jnp.concatenate([block2[1], token1[2], pair0[3]], axis=1), 0)

    mine1 = middle(total1, after(arrived1, far0))
    other1 = send(mine1, core=1)
    pair1 = pair_rows(mine1, other1)
    got1 = exchange(pair1[3], 0)
    result01 = back(
        after(jnp.concatenate([mine0, mine1], axis=1), pair1[3]), jnp.concatenate([other0, other1], axis=1), weights
    )
    result0, result1 = result01[:, :96], result01[:, 96:].astype(BF)
    mine2 = middle(total2, after(arrived2, pair1[3]))
    other2 = send(after(mine2, result1), core=1)
    pair2 = pair_rows(after(mine2, far1, far0), other2)
    got2 = exchange(pair2[3], 0)

    cot_pair = jnp.concatenate([cot0, block2[1], far0[:, :1536], far1[:, :1536]], axis=0)
    token_own = jnp.concatenate([token0[0], token1[0], far0[:, 1536:1920], far1[:, 1536:1920]], axis=0)
    token_second = jnp.concatenate([token0[1], token1[1], far0[:, 1920:], far1[:, 1920:2304]], axis=0)
    cot_pair, token_own, token_second = lax.optimization_barrier((cot_pair, token_own, token_second))

    pairs = (pair0, pair1, pair2)
    gots = (far1[:, 2304:], got1, got2)

    def joined(i, cols):
        return jnp.concatenate([p[i] for p in pairs] + [p[:, cols] for p in gots], axis=0)

    act_own = joined(0, slice(0, 384))
    act_second = joined(1, slice(384, 768))
    grad_pair = joined(2, slice(768, 2304))
    act_own, act_second, grad_pair = lax.optimization_barrier((act_own, act_second, grad_pair))
    out_sent = dot(act_second, cot_pair, (0, 0)).astype(BF)
    out_kept, in_kept = lax.optimization_barrier(
        (dot(act_own, cot_pair, (0, 0)), dot(token_own, grad_pair, (0, 0)))
    )
    in_sent = dot(after(token_second, out_kept, in_kept), grad_pair, (0, 0)).astype(BF)
    grad_w_out = (out_kept + exchange(out_sent, 1).astype(F32)).astype(BF)
    grad_w_in = (in_kept + exchange(in_sent, 1).astype(F32)).astype(BF)

    result2 = back(after(mine2, pair2[3]), other2, weights).astype(BF)
    total = result0
    for part in (send(result1[:, :96], x=1), send(result1[:, 96:], x=3), send(result2, x=2)):
        total = total + part.astype(F32)
    total = after(total, out_sent, in_sent)
    arrived = [send(total[:, 24 * k : 24 * k + 24].astype(BF), lo=k) for k in (1, 2, 3)]

    sums = total[:, :24]
    for part in arrived:
        sums = sums + after(part, grad_w_out, grad_w_in).astype(F32)
    layer_out = sums[0].astype(BF)
    grad_tokens = sums[1].astype(BF)
    return (layer_out, grad_tokens, grad_w_in, grad_w_out)


def solution(mesh):
    return jax.shard_map(
        local,
        mesh=mesh,
        in_specs=(
            P(("depth", "col"), "row"),
            P("row", "col"),
            P("col", "row"),
            P(("depth", "col"), "row"),
        ),
        out_specs=(
            P(("depth", "col"), "row"),
            P(("depth", "col"), "row"),
            P(("row", "depth"), "col"),
            P(("col", "depth"), "row"),
        ),
        check_vma=False,
    )
```

profile of v0, /device:TPU:32, one launch (start us, length us, event | category | flops | bytes accessed | tf_op | source)
XLA Modules:
  0.0 140.7 jit_solution(11984387601310695617)
XLA Ops:
  0.6 1.7 %pad_maximum_fusion.14 = bf16[2,24,1536]{2,1,0:T(8,128)(2,1)} fusion(bf16[1,24,1536]{2,1,0:T(8,128)(2,1)} %bitcast.179, bf16[1,24,1536]{2,1,0:T(8,128)(2,1)} %bitcast.181), kind=kLoop, calls=%fused_computation.190 | loop fusion | flops 73728 | bytes 294912 | tf_op jit(solution)/shard_map/stack | solution.py:94
  2.3 1.9 %collective-permute-start.2 = (bf16[2,24,1536]{2,1,0:T(8,128)(2,1)}, bf16[2,24,1536]{2,1,0:T(8,128)(2,1)S(1)}, u32[]{:S(2)}, u32[]{:S(2)}) collective-permute-start(bf16[2,24,1536]{2,1,0:T(8,128)(2,1)} %pad_maximum_fusion.14), channel_id=1, source_target_pairs={{0,16},{1,17},{2,18},{3,19},{4,20},{5,21},{6,22},{7,23},{8,24},{9,... | collective-permute-start | bytes 442376 | tf_op jit(solution)/shard_map/ppermute | solution.py:35
  4.2 2.3 %collective-permute-start.1 = (bf16[2,24,1536]{2,1,0:T(8,128)(2,1)}, bf16[2,24,1536]{2,1,0:T(8,128)(2,1)S(1)}, u32[]{:S(2)}, u32[]{:S(2)}) collective-permute-start(bf16[2,24,1536]{2,1,0:T(8,128)(2,1)} %pad_maximum_fusion.14), channel_id=1, source_target_pairs={{0,32},{1,33},{2,34},{3,35},{4,36},{5,37},{6,38},{7,39},{8,40},{9,... | collective-permute-start | bytes 442376 | tf_op jit(solution)/shard_map/ppermute | solution.py:35
  6.5 1.1 collective-permute-start
  7.6 4.2 %constant_dynamic-slice_fusion.4 = (bf16[1536,768]{1,0:T(8,128)(2,1)S(1)}, bf16[1536,768]{1,0:T(8,128)(2,1)}) fusion(bf16[1536,1536]{1,0:T(8,128)(2,1)} %param.5, s32[]{:T(128)S(6)} %select_n.141, s32[]{:T(128)S(6)} %select_n.140), kind=kLoop, calls=%fused_computation.238 | loop fusion | bytes 9437192 | tf_op jit(solution)/shard_map/dynamic_slice | solution.py:86
  11.9 2.5 %constant_dynamic-slice_fusion.2 = (bf16[768,1536]{1,0:T(8,128)(2,1)}, bf16[768,1536]{1,0:T(8,128)(2,1)}) fusion(bf16[1536,1536]{1,0:T(8,128)(2,1)S(1)} %bitcast.178, s32[]{:T(128)S(6)} %select_n.141, s32[]{:T(128)S(6)} %select_n.140), kind=kLoop, calls=%fused_computation.236 | loop fusion | bytes 9437192 | tf_op jit(solution)/shard_map/dynamic_slice | solution.py:88
  15.1 2.0 %collective-permute-done.1 = bf16[2,24,1536]{2,1,0:T(8,128)(2,1)S(1)} collective-permute-done((bf16[2,24,1536]{2,1,0:T(8,128)(2,1)}, bf16[2,24,1536]{2,1,0:T(8,128)(2,1)S(1)}, u32[]{:S(2)}, u32[]{:S(2)}) %collective-permute-start.1) | collective-permute-done | bytes 147488 | tf_op jit(solution)/shard_map/ppermute | solution.py:35
  17.1 2.0 %collective-permute-done = bf16[2,24,1536]{2,1,0:T(8,128)(2,1)S(1)} collective-permute-done((bf16[2,24,1536]{2,1,0:T(8,128)(2,1)}, bf16[2,24,1536]{2,1,0:T(8,128)(2,1)S(1)}, u32[]{:S(2)}, u32[]{:S(2)}) %collective-permute-start) | collective-permute-done | bytes 147488 | tf_op jit(solution)/shard_map/ppermute | solution.py:35
  19.2 1.6 %collective-permute-start.6 = (bf16[2,96,1536]{2,1,0:T(8,128)(2,1)S(1)}, bf16[2,96,1536]{2,1,0:T(8,128)(2,1)S(1)}, u32[]{:S(2)}, u32[]{:S(2)}) collective-permute-start(bf16[2,96,1536]{2,1,0:T(8,128)(2,1)S(1)} %pad_maximum_fusion.3), channel_id=1, source_target_pairs={{0,4},{1,5},{2,6},{3,7},{4,8},{5,9},{6,10},{7,11},{8,12},{9,13},{1... | collective-permute-start | bytes 1769480 | tf_op jit(solution)/shard_map/ppermute | solution.py:35
  20.8 1.7 %collective-permute-start.5 = (bf16[2,96,1536]{2,1,0:T(8,128)(2,1)S(1)}, bf16[2,96,1536]{2,1,0:T(8,128)(2,1)S(1)}, u32[]{:S(2)}, u32[]{:S(2)}) collective-permute-start(bf16[2,96,1536]{2,1,0:T(8,128)(2,1)S(1)} %pad_maximum_fusion.3), channel_id=1, source_target_pairs={{0,12},{1,13},{2,14},{3,15},{4,0},{5,1},{6,2},{7,3},{8,4},{9,5},{1... | collective-permute-start | bytes 1769480 | tf_op jit(solution)/shard_map/ppermute | solution.py:35
  25.8 0.8 convolution_bitcast_fusion.4
  26.7 6.1 %collective-permute-start.4 = (bf16[2,96,768]{2,1,0:T(8,128)(2,1)S(1)}, bf16[2,96,768]{2,1,0:T(8,128)(2,1)S(1)}, u32[]{:S(2)}, u32[]{:S(2)}) collective-permute-start(bf16[2,96,768]{2,1,0:T(8,128)(2,1)S(1)} %fusion.39), channel_id=1, source_target_pairs={{0,128},{1,129},{2,130},{3,131},{4,132},{5,133},{6,134},{7,135},{8... | collective-permute-start | bytes 884744 | tf_op jit(solution)/shard_map/ppermute | solution.py:35
  32.8 3.0 %collective-permute-done.5 = bf16[2,96,1536]{2,1,0:T(8,128)(2,1)S(1)} collective-permute-done((bf16[2,96,1536]{2,1,0:T(8,128)(2,1)S(1)}, bf16[2,96,1536]{2,1,0:T(8,128)(2,1)S(1)}, u32[]{:S(2)}, u32[]{:S(2)}) %collective-permute-start.5) | collective-permute-done | bytes 589856 | tf_op jit(solution)/shard_map/ppermute | solution.py:35
  36.6 0.9 fusion.12
  38.1 0.9 convolution_bitcast_fusion
  39.4 1.8 %collective-permute-done.7 = bf16[2,192,768]{2,1,0:T(8,128)(2,1)S(1)} collective-permute-done((bf16[2,192,768]{2,1,0:T(8,128)(2,1)S(1)}, bf16[2,192,768]{2,1,0:T(8,128)(2,1)S(1)}, u32[]{:S(2)}, u32[]{:S(2)}) %collective-permute-start.7) | collective-permute-done | bytes 589856 | tf_op jit(solution)/shard_map/ppermute | solution.py:35
  41.4 3.0 %collective-permute-start.8 = (bf16[96,1536]{1,0:T(8,128)(2,1)S(1)}, bf16[96,1536]{1,0:T(8,128)(2,1)S(1)}, u32[]{:S(2)}, u32[]{:S(2)}) collective-permute-start(bf16[96,1536]{1,0:T(8,128)(2,1)S(1)} %slice_bitcast_fusion.11), channel_id=1, source_target_pairs={{0,12},{1,13},{2,14},{3,15},{4,0},{5,1},{6,2},{7,3},{8,4},{9,5},{1... | collective-permute-start | bytes 884744 | tf_op jit(solution)/shard_map/ppermute | solution.py:35
  44.5 6.1 %collective-permute-start.11 = (bf16[2,192,768]{2,1,0:T(8,128)(2,1)S(1)}, bf16[2,192,768]{2,1,0:T(8,128)(2,1)S(1)}, u32[]{:S(2)}, u32[]{:S(2)}) collective-permute-start(bf16[2,192,768]{2,1,0:T(8,128)(2,1)S(1)} %fusion.17), channel_id=1, source_target_pairs={{0,128},{1,129},{2,130},{3,131},{4,132},{5,133},{6,134},{7,135},{8... | collective-permute-start | bytes 1769480 | tf_op jit(solution)/shard_map/ppermute | solution.py:35
  50.6 1.6 %collective-permute-start.12 = (bf16[288,2304]{1,0:T(8,128)(2,1)S(1)}, bf16[288,2304]{1,0:T(8,128)(2,1)S(1)}, u32[]{:S(2)}, u32[]{:S(2)}) collective-permute-start(bf16[288,2304]{1,0:T(8,128)(2,1)S(1)} %pad_maximum_fusion.1), channel_id=1, source_target_pairs={{0,1},{1,0},{2,3},{3,2},{4,5},{5,4},{6,7},{7,6},{8,9},{9,8},{10,11... | collective-permute-start | bytes 3981320 | tf_op jit(solution)/shard_map/ppermute | solution.py:45
  52.7 1.7 %collective-permute-done.9 = bf16[96,1536]{1,0:T(8,128)(2,1)S(1)} collective-permute-done((bf16[96,1536]{1,0:T(8,128)(2,1)S(1)}, bf16[96,1536]{1,0:T(8,128)(2,1)S(1)}, u32[]{:S(2)}, u32[]{:S(2)}) %collective-permute-start.9) | collective-permute-done | bytes 294944 | tf_op jit(solution)/shard_map/ppermute | solution.py:35
  54.4 0.8 fusion.16
  55.9 0.8 convolution_bitcast_fusion.2
  58.0 5.9 %collective-permute-start.17 = (bf16[2,96,768]{2,1,0:T(8,128)(2,1)S(1)}, bf16[2,96,768]{2,1,0:T(8,128)(2,1)S(1)}, u32[]{:S(2)}, u32[]{:S(2)}) collective-permute-start(bf16[2,96,768]{2,1,0:T(8,128)(2,1)S(1)} %fusion.38), channel_id=1, source_target_pairs={{0,128},{1,129},{2,130},{3,131},{4,132},{5,133},{6,134},{7,135},{8... | collective-permute-start | bytes 884744 | tf_op jit(solution)/shard_map/ppermute | solution.py:35
  64.4 1.7 %collective-permute-start.18 = (bf16[96,4608]{1,0:T(8,128)(2,1)S(1)}, bf16[96,4608]{1,0:T(8,128)(2,1)S(1)}, u32[]{:S(2)}, u32[]{:S(2)}) collective-permute-start(bf16[96,4608]{1,0:T(8,128)(2,1)S(1)} %get-tuple-element.56), channel_id=1, source_target_pairs={{0,1},{1,0},{2,3},{3,2},{4,5},{5,4},{6,7},{7,6},{8,9},{9,8},{10,11... | collective-permute-start | bytes 2654216 | tf_op jit(solution)/shard_map/ppermute | solution.py:45
  66.1 16.6 %collective-permute-done.11 = bf16[2,192,768]{2,1,0:T(8,128)(2,1)S(1)} collective-permute-done((bf16[2,192,768]{2,1,0:T(8,128)(2,1)S(1)}, bf16[2,192,768]{2,1,0:T(8,128)(2,1)S(1)}, u32[]{:S(2)}, u32[]{:S(2)}) %collective-permute-start.11) | collective-permute-done | bytes 589856 | tf_op jit(solution)/shard_map/ppermute | solution.py:35
  83.8 1.8 %collective-permute-done.13 = bf16[2,192,768]{2,1,0:T(8,128)(2,1)S(1)} collective-permute-done((bf16[2,192,768]{2,1,0:T(8,128)(2,1)S(1)}, bf16[2,192,768]{2,1,0:T(8,128)(2,1)S(1)}, u32[]{:S(2)}, u32[]{:S(2)}) %collective-permute-start.13) | collective-permute-done | bytes 589856 | tf_op jit(solution)/shard_map/ppermute | solution.py:35
  86.5 1.7 %collective-permute-start.21 = (bf16[192,2304]{1,0:T(8,128)(2,1)S(1)}, bf16[192,2304]{1,0:T(8,128)(2,1)S(1)}, u32[]{:S(2)}, u32[]{:S(2)}) collective-permute-start(bf16[192,2304]{1,0:T(8,128)(2,1)S(1)} %pad_maximum_fusion.2), channel_id=1, source_target_pairs={{0,1},{1,0},{2,3},{3,2},{4,5},{5,4},{6,7},{7,6},{8,9},{9,8},{10,11... | collective-permute-start | bytes 2654216 | tf_op jit(solution)/shard_map/ppermute | solution.py:45
  89.9 0.9 fusion.32
  90.8 0.8 fusion.34
  91.7 0.9 fusion.2
  92.6 0.8 fusion.1
  94.4 3.0 %collective-permute-start.16 = (bf16[2,96,1536]{2,1,0:T(8,128)(2,1)S(1)}, bf16[2,96,1536]{2,1,0:T(8,128)(2,1)S(1)}, u32[]{:S(2)}, u32[]{:S(2)}) collective-permute-start(bf16[2,96,1536]{2,1,0:T(8,128)(2,1)S(1)} %get-tuple-element.68), channel_id=1, source_target_pairs={{0,12},{1,13},{2,14},{3,15},{4,0},{5,1},{6,2},{7,3},{8,4},{9,5},{1... | collective-permute-start | bytes 1769480 | tf_op jit(solution)/shard_map/ppermute | solution.py:35
  97.7 1.1 collective-permute-start.22
  100.2 0.8 fusion.5
  101.7 1.2 collective-permute-start.20
  103.3 2.9 %collective-permute-done.22 = bf16[96,2304]{1,0:T(8,128)(2,1)S(1)} collective-permute-done((bf16[96,2304]{1,0:T(8,128)(2,1)S(1)}, bf16[96,2304]{1,0:T(8,128)(2,1)S(1)}, u32[]{:S(2)}, u32[]{:S(2)}) %collective-permute-start.22) | collective-permute-done | bytes 442400 | tf_op jit(solution)/shard_map/ppermute | solution.py:45
  106.2 1.1 convolution_convert_fusion.1
  107.3 1.1 fusion.97
  108.4 2.6 %collective-permute-start.24 = (bf16[384,1536]{1,0:T(8,128)(2,1)S(1)}, bf16[384,1536]{1,0:T(8,128)(2,1)S(1)}, u32[]{:S(2)}, u32[]{:S(2)}) collective-permute-start(bf16[384,1536]{1,0:T(8,128)(2,1)S(1)} %convolution_convert_fusion.1), channel_id=1, source_target_pairs={{0,3},{1,2},{2,1},{3,0},{4,7},{5,6},{6,5},{7,4},{8,11},{9,10},{10,... | collective-permute-start | bytes 3538952 | tf_op jit(solution)/shard_map/ppermute | solution.py:45
  111.0 1.1 fusion.98
  112.1 1.1 convolution_convert_fusion
  113.2 0.9 collective-permute-start.25
  114.1 8.5 %collective-permute-done.16 = bf16[2,96,1536]{2,1,0:T(8,128)(2,1)S(1)} collective-permute-done((bf16[2,96,1536]{2,1,0:T(8,128)(2,1)S(1)}, bf16[2,96,1536]{2,1,0:T(8,128)(2,1)S(1)}, u32[]{:S(2)}, u32[]{:S(2)}) %collective-permute-start.16) | collective-permute-done | bytes 589856 | tf_op jit(solution)/shard_map/ppermute | solution.py:35
  122.6 1.8 %collective-permute-done.20 = bf16[2,96,1536]{2,1,0:T(8,128)(2,1)S(1)} collective-permute-done((bf16[2,96,1536]{2,1,0:T(8,128)(2,1)S(1)}, bf16[2,96,1536]{2,1,0:T(8,128)(2,1)S(1)}, u32[]{:S(2)}, u32[]{:S(2)}) %collective-permute-start.20) | collective-permute-done | bytes 589856 | tf_op jit(solution)/shard_map/ppermute | solution.py:35
  124.8 2.0 %collective-permute-start.27 = (bf16[2,24,1536]{2,1,0:T(8,128)(2,1)S(1)}, bf16[2,24,1536]{2,1,0:T(8,128)(2,1)S(1)}, u32[]{:S(2)}, u32[]{:S(2)}) collective-permute-start(bf16[2,24,1536]{2,1,0:T(8,128)(2,1)S(1)} %get-tuple-element.88), channel_id=1, source_target_pairs={{0,48},{1,49},{2,50},{3,51},{4,52},{5,53},{6,54},{7,55},{8,56},{9,... | collective-permute-start | bytes 442376 | tf_op jit(solution)/shard_map/ppermute | solution.py:35
  126.9 1.4 add_convert_fusion.1
  128.3 10.3 %collective-permute-done.25 = bf16[384,1536]{1,0:T(8,128)(2,1)S(1)} collective-permute-done((bf16[384,1536]{1,0:T(8,128)(2,1)S(1)}, bf16[384,1536]{1,0:T(8,128)(2,1)S(1)}, u32[]{:S(2)}, u32[]{:S(2)}) %collective-permute-start.25) | collective-permute-done | bytes 1179680 | tf_op jit(solution)/shard_map/ppermute | solution.py:45
  138.5 1.4 add_convert_fusion
  (121 shorter events, 17.4 us)
Async XLA Ops:
  0.6 11.2 %slice-start = ((s8[4718592]{0:T(1024)(128)(4,1)}), s8[524288]{0:T(1024)(128)(4,1)S(1)}, s32[]{:S(2)}) async-start(s8[4718592]{0:T(1024)(128)(4,1)} %bitcast.177), calls=%async_computation | async-start | bytes 1048576
  2.3 12.8 %collective-permute-start.2 = (bf16[2,24,1536]{2,1,0:T(8,128)(2,1)}, bf16[2,24,1536]{2,1,0:T(8,128)(2,1)S(1)}, u32[]{:S(2)}, u32[]{:S(2)}) collective-permute-start(bf16[2,24,1536]{2,1,0:T(8,128)(2,1)} %pad_maximum_fusion.14), channel_id=1, source_target_pairs={{0,16},{1,17},{2,18},{3,19},{4,20},{5,21},{6,22},{7,23},{8,24},{9,... | collective-permute-start | bytes 442376 | tf_op jit(solution)/shard_map/ppermute | solution.py:35
  4.2 12.9 %collective-permute-start.1 = (bf16[2,24,1536]{2,1,0:T(8,128)(2,1)}, bf16[2,24,1536]{2,1,0:T(8,128)(2,1)S(1)}, u32[]{:S(2)}, u32[]{:S(2)}) collective-permute-start(bf16[2,24,1536]{2,1,0:T(8,128)(2,1)} %pad_maximum_fusion.14), channel_id=1, source_target_pairs={{0,32},{1,33},{2,34},{3,35},{4,36},{5,37},{6,38},{7,39},{8,40},{9,... | collective-permute-start | bytes 442376 | tf_op jit(solution)/shard_map/ppermute | solution.py:35
  6.5 12.6 %collective-permute-start = (bf16[2,24,1536]{2,1,0:T(8,128)(2,1)}, bf16[2,24,1536]{2,1,0:T(8,128)(2,1)S(1)}, u32[]{:S(2)}, u32[]{:S(2)}) collective-permute-start(bf16[2,24,1536]{2,1,0:T(8,128)(2,1)} %pad_maximum_fusion.14), channel_id=1, source_target_pairs={{0,48},{1,49},{2,50},{3,51},{4,52},{5,53},{6,54},{7,55},{8,56},{9,... | collective-permute-start | bytes 442376 | tf_op jit(solution)/shard_map/ppermute | solution.py:35
  7.6 4.2 %slice-start.1 = ((s8[4718592]{0:T(1024)(128)(4,1)}), s8[4194304]{0:T(1024)(128)(4,1)S(1)}, s32[]{:S(2)}) async-start(s8[4718592]{0:T(1024)(128)(4,1)} %bitcast.177), calls=%async_computation.1 | async-start | bytes 8388608
  11.8 7.3 %copy-start.3 = (bf16[24,1536]{1,0:T(8,128)(2,1)S(1)}, bf16[24,1536]{1,0:T(8,128)(2,1)}, u32[]{:S(2)}) copy-start(bf16[24,1536]{1,0:T(8,128)(2,1)} %param.7) | copy-start | bytes 221188
  11.8 7.3 %copy-start.4 = (bf16[24,1536]{1,0:T(8,128)(2,1)S(1)}, bf16[24,1536]{1,0:T(8,128)(2,1)}, u32[]{:S(2)}) copy-start(bf16[24,1536]{1,0:T(8,128)(2,1)} %param.4) | copy-start | bytes 221188
  19.2 3.9 %copy-start = (bf16[768,1536]{1,0:T(8,128)(2,1)S(1)}, bf16[768,1536]{1,0:T(8,128)(2,1)}, u32[]{:S(2)}) copy-start(bf16[768,1536]{1,0:T(8,128)(2,1)} %get-tuple-element.33) | copy-start | bytes 7077892
  19.2 16.6 %collective-permute-start.6 = (bf16[2,96,1536]{2,1,0:T(8,128)(2,1)S(1)}, bf16[2,96,1536]{2,1,0:T(8,128)(2,1)S(1)}, u32[]{:S(2)}, u32[]{:S(2)}) collective-permute-start(bf16[2,96,1536]{2,1,0:T(8,128)(2,1)S(1)} %pad_maximum_fusion.3), channel_id=1, source_target_pairs={{0,4},{1,5},{2,6},{3,7},{4,8},{5,9},{6,10},{7,11},{8,12},{9,13},{1... | collective-permute-start | bytes 1769480 | tf_op jit(solution)/shard_map/ppermute | solution.py:35
  20.8 15.0 %collective-permute-start.5 = (bf16[2,96,1536]{2,1,0:T(8,128)(2,1)S(1)}, bf16[2,96,1536]{2,1,0:T(8,128)(2,1)S(1)}, u32[]{:S(2)}, u32[]{:S(2)}) collective-permute-start(bf16[2,96,1536]{2,1,0:T(8,128)(2,1)S(1)} %pad_maximum_fusion.3), channel_id=1, source_target_pairs={{0,12},{1,13},{2,14},{3,15},{4,0},{5,1},{6,2},{7,3},{8,4},{9,5},{1... | collective-permute-start | bytes 1769480 | tf_op jit(solution)/shard_map/ppermute | solution.py:35
  23.1 1.7 %copy-start.2 = (bf16[1536,768]{1,0:T(8,128)(2,1)S(1)}, bf16[1536,768]{1,0:T(8,128)(2,1)}, u32[]{:S(2)}) copy-start(bf16[1536,768]{1,0:T(8,128)(2,1)} %get-tuple-element.30) | copy-start | bytes 7077892
  23.9 1.9 %copy-start.1 = (bf16[768,1536]{1,0:T(8,128)(2,1)S(1)}, bf16[768,1536]{1,0:T(8,128)(2,1)}, u32[]{:S(2)}) copy-start(bf16[768,1536]{1,0:T(8,128)(2,1)} %get-tuple-element.31) | copy-start | bytes 7077892
  24.0 2.6 %collective-permute-start.3 = (bf16[2,96,768]{2,1,0:T(8,128)(2,1)S(1)}, bf16[2,96,768]{2,1,0:T(8,128)(2,1)S(1)}, u32[]{:S(2)}, u32[]{:S(2)}) collective-permute-start(bf16[2,96,768]{2,1,0:T(8,128)(2,1)S(1)} %pad_maximum_fusion.10), channel_id=1, source_target_pairs={{0,64},{1,65},{2,66},{3,67},{4,68},{5,69},{6,70},{7,71},{8,72},{9,... | collective-permute-start | bytes 884744 | tf_op jit(solution)/shard_map/ppermute | solution.py:35
  26.7 30.3 %collective-permute-start.4 = (bf16[2,96,768]{2,1,0:T(8,128)(2,1)S(1)}, bf16[2,96,768]{2,1,0:T(8,128)(2,1)S(1)}, u32[]{:S(2)}, u32[]{:S(2)}) collective-permute-start(bf16[2,96,768]{2,1,0:T(8,128)(2,1)S(1)} %fusion.39), channel_id=1, source_target_pairs={{0,128},{1,129},{2,130},{3,131},{4,132},{5,133},{6,134},{7,135},{8... | collective-permute-start | bytes 884744 | tf_op jit(solution)/shard_map/ppermute | solution.py:35
  39.1 2.1 %collective-permute-start.7 = (bf16[2,192,768]{2,1,0:T(8,128)(2,1)S(1)}, bf16[2,192,768]{2,1,0:T(8,128)(2,1)S(1)}, u32[]{:S(2)}, u32[]{:S(2)}) collective-permute-start(bf16[2,192,768]{2,1,0:T(8,128)(2,1)S(1)} %pad_maximum_fusion.4), channel_id=1, source_target_pairs={{0,64},{1,65},{2,66},{3,67},{4,68},{5,69},{6,70},{7,71},{8,72},{9,... | collective-permute-start | bytes 1769480 | tf_op jit(solution)/shard_map/ppermute | solution.py:35
  41.4 10.8 %collective-permute-start.8 = (bf16[96,1536]{1,0:T(8,128)(2,1)S(1)}, bf16[96,1536]{1,0:T(8,128)(2,1)S(1)}, u32[]{:S(2)}, u32[]{:S(2)}) collective-permute-start(bf16[96,1536]{1,0:T(8,128)(2,1)S(1)} %slice_bitcast_fusion.11), channel_id=1, source_target_pairs={{0,12},{1,13},{2,14},{3,15},{4,0},{5,1},{6,2},{7,3},{8,4},{9,5},{1... | collective-permute-start | bytes 884744 | tf_op jit(solution)/shard_map/ppermute | solution.py:35
  44.4 10.0 %collective-permute-start.9 = (bf16[96,1536]{1,0:T(8,128)(2,1)S(1)}, bf16[96,1536]{1,0:T(8,128)(2,1)S(1)}, u32[]{:S(2)}, u32[]{:S(2)}) collective-permute-start(bf16[96,1536]{1,0:T(8,128)(2,1)S(1)} %slice_bitcast_fusion.10), channel_id=1, source_target_pairs={{0,4},{1,5},{2,6},{3,7},{4,8},{5,9},{6,10},{7,11},{8,12},{9,13},{1... | collective-permute-start | bytes 884744 | tf_op jit(solution)/shard_map/ppermute | solution.py:35
  44.5 38.1 %collective-permute-start.11 = (bf16[2,192,768]{2,1,0:T(8,128)(2,1)S(1)}, bf16[2,192,768]{2,1,0:T(8,128)(2,1)S(1)}, u32[]{:S(2)}, u32[]{:S(2)}) collective-permute-start(bf16[2,192,768]{2,1,0:T(8,128)(2,1)S(1)} %fusion.17), channel_id=1, source_target_pairs={{0,128},{1,129},{2,130},{3,131},{4,132},{5,133},{6,134},{7,135},{8... | collective-permute-start | bytes 1769480 | tf_op jit(solution)/shard_map/ppermute | solution.py:35
  50.6 32.1 %collective-permute-start.12 = (bf16[288,2304]{1,0:T(8,128)(2,1)S(1)}, bf16[288,2304]{1,0:T(8,128)(2,1)S(1)}, u32[]{:S(2)}, u32[]{:S(2)}) collective-permute-start(bf16[288,2304]{1,0:T(8,128)(2,1)S(1)} %pad_maximum_fusion.1), channel_id=1, source_target_pairs={{0,1},{1,0},{2,3},{3,2},{4,5},{5,4},{6,7},{7,6},{8,9},{9,8},{10,11... | collective-permute-start | bytes 3981320 | tf_op jit(solution)/shard_map/ppermute | solution.py:45
  55.3 1.7 %collective-permute-start.10 = (bf16[2,96,768]{2,1,0:T(8,128)(2,1)S(1)}, bf16[2,96,768]{2,1,0:T(8,128)(2,1)S(1)}, u32[]{:S(2)}, u32[]{:S(2)}) collective-permute-start(bf16[2,96,768]{2,1,0:T(8,128)(2,1)S(1)} %pad_maximum_fusion.11), channel_id=1, source_target_pairs={{0,64},{1,65},{2,66},{3,67},{4,68},{5,69},{6,70},{7,71},{8,72},{9,... | collective-permute-start | bytes 884744 | tf_op jit(solution)/shard_map/ppermute | solution.py:35
  57.4 6.5 %collective-permute-start.14 = (bf16[2,96,768]{2,1,0:T(8,128)(2,1)S(1)}, bf16[2,96,768]{2,1,0:T(8,128)(2,1)S(1)}, u32[]{:S(2)}, u32[]{:S(2)}) collective-permute-start(bf16[2,96,768]{2,1,0:T(8,128)(2,1)S(1)} %pad_maximum_fusion.12), channel_id=1, source_target_pairs={{0,64},{1,65},{2,66},{3,67},{4,68},{5,69},{6,70},{7,71},{8,72},{9,... | collective-permute-start | bytes 884744 | tf_op jit(solution)/shard_map/ppermute | solution.py:35
  58.0 30.9 %collective-permute-start.17 = (bf16[2,96,768]{2,1,0:T(8,128)(2,1)S(1)}, bf16[2,96,768]{2,1,0:T(8,128)(2,1)S(1)}, u32[]{:S(2)}, u32[]{:S(2)}) collective-permute-start(bf16[2,96,768]{2,1,0:T(8,128)(2,1)S(1)} %fusion.38), channel_id=1, source_target_pairs={{0,128},{1,129},{2,130},{3,131},{4,132},{5,133},{6,134},{7,135},{8... | collective-permute-start | bytes 884744 | tf_op jit(solution)/shard_map/ppermute | solution.py:35
  64.4 27.3 %collective-permute-start.18 = (bf16[96,4608]{1,0:T(8,128)(2,1)S(1)}, bf16[96,4608]{1,0:T(8,128)(2,1)S(1)}, u32[]{:S(2)}, u32[]{:S(2)}) collective-permute-start(bf16[96,4608]{1,0:T(8,128)(2,1)S(1)} %get-tuple-element.56), channel_id=1, source_target_pairs={{0,1},{1,0},{2,3},{3,2},{4,5},{5,4},{6,7},{7,6},{8,9},{9,8},{10,11... | collective-permute-start | bytes 2654216 | tf_op jit(solution)/shard_map/ppermute | solution.py:45
  83.5 2.1 %collective-permute-start.13 = (bf16[2,192,768]{2,1,0:T(8,128)(2,1)S(1)}, bf16[2,192,768]{2,1,0:T(8,128)(2,1)S(1)}, u32[]{:S(2)}, u32[]{:S(2)}) collective-permute-start(bf16[2,192,768]{2,1,0:T(8,128)(2,1)S(1)} %pad_maximum_fusion.5), channel_id=1, source_target_pairs={{0,64},{1,65},{2,66},{3,67},{4,68},{5,69},{6,70},{7,71},{8,72},{9,... | collective-permute-start | bytes 1769480 | tf_op jit(solution)/shard_map/ppermute | solution.py:35
  86.5 16.7 %collective-permute-start.21 = (bf16[192,2304]{1,0:T(8,128)(2,1)S(1)}, bf16[192,2304]{1,0:T(8,128)(2,1)S(1)}, u32[]{:S(2)}, u32[]{:S(2)}) collective-permute-start(bf16[192,2304]{1,0:T(8,128)(2,1)S(1)} %pad_maximum_fusion.2), channel_id=1, source_target_pairs={{0,1},{1,0},{2,3},{3,2},{4,5},{5,4},{6,7},{7,6},{8,9},{9,8},{10,11... | collective-permute-start | bytes 2654216 | tf_op jit(solution)/shard_map/ppermute | solution.py:45
  89.3 8.2 %collective-permute-start.19 = (bf16[2,96,768]{2,1,0:T(8,128)(2,1)S(1)}, bf16[2,96,768]{2,1,0:T(8,128)(2,1)S(1)}, u32[]{:S(2)}, u32[]{:S(2)}) collective-permute-start(bf16[2,96,768]{2,1,0:T(8,128)(2,1)S(1)} %pad_maximum_fusion.13), channel_id=1, source_target_pairs={{0,64},{1,65},{2,66},{3,67},{4,68},{5,69},{6,70},{7,71},{8,72},{9,... | collective-permute-start | bytes 884744 | tf_op jit(solution)/shard_map/ppermute | solution.py:35
  93.9 20.2 %collective-permute-start.15 = (bf16[2,96,1536]{2,1,0:T(8,128)(2,1)S(1)}, bf16[2,96,1536]{2,1,0:T(8,128)(2,1)S(1)}, u32[]{:S(2)}, u32[]{:S(2)}) collective-permute-start(bf16[2,96,1536]{2,1,0:T(8,128)(2,1)S(1)} %get-tuple-element.67), channel_id=1, source_target_pairs={{0,4},{1,5},{2,6},{3,7},{4,8},{5,9},{6,10},{7,11},{8,12},{9,13},{1... | collective-permute-start | bytes 1769480 | tf_op jit(solution)/shard_map/ppermute | solution.py:35
  94.4 28.2 %collective-permute-start.16 = (bf16[2,96,1536]{2,1,0:T(8,128)(2,1)S(1)}, bf16[2,96,1536]{2,1,0:T(8,128)(2,1)S(1)}, u32[]{:S(2)}, u32[]{:S(2)}) collective-permute-start(bf16[2,96,1536]{2,1,0:T(8,128)(2,1)S(1)} %get-tuple-element.68), channel_id=1, source_target_pairs={{0,12},{1,13},{2,14},{3,15},{4,0},{5,1},{6,2},{7,3},{8,4},{9,5},{1... | collective-permute-start | bytes 1769480 | tf_op jit(solution)/shard_map/ppermute | solution.py:35
  97.7 8.4 %collective-permute-start.22 = (bf16[96,2304]{1,0:T(8,128)(2,1)S(1)}, bf16[96,2304]{1,0:T(8,128)(2,1)S(1)}, u32[]{:S(2)}, u32[]{:S(2)}) collective-permute-start(bf16[96,2304]{1,0:T(8,128)(2,1)S(1)} %pad_maximum_fusion.9), channel_id=1, source_target_pairs={{0,1},{1,0},{2,3},{3,2},{4,5},{5,4},{6,7},{7,6},{8,9},{9,8},{10,11... | collective-permute-start | bytes 1327112 | tf_op jit(solution)/shard_map/ppermute | solution.py:45
  101.7 22.7 %collective-permute-start.20 = (bf16[2,96,1536]{2,1,0:T(8,128)(2,1)S(1)}, bf16[2,96,1536]{2,1,0:T(8,128)(2,1)S(1)}, u32[]{:S(2)}, u32[]{:S(2)}) collective-permute-start(bf16[2,96,1536]{2,1,0:T(8,128)(2,1)S(1)} %pad_maximum_fusion.6), channel_id=1, source_target_pairs={{0,8},{1,9},{2,10},{3,11},{4,12},{5,13},{6,14},{7,15},{8,0},{9,1},... | collective-permute-start | bytes 1769480 | tf_op jit(solution)/shard_map/ppermute | solution.py:35
  108.4 18.5 %collective-permute-start.24 = (bf16[384,1536]{1,0:T(8,128)(2,1)S(1)}, bf16[384,1536]{1,0:T(8,128)(2,1)S(1)}, u32[]{:S(2)}, u32[]{:S(2)}) collective-permute-start(bf16[384,1536]{1,0:T(8,128)(2,1)S(1)} %convolution_convert_fusion.1), channel_id=1, source_target_pairs={{0,3},{1,2},{2,1},{3,0},{4,7},{5,6},{6,5},{7,4},{8,11},{9,10},{10,... | collective-permute-start | bytes 3538952 | tf_op jit(solution)/shard_map/ppermute | solution.py:45
  113.2 25.3 %collective-permute-start.25 = (bf16[384,1536]{1,0:T(8,128)(2,1)S(1)}, bf16[384,1536]{1,0:T(8,128)(2,1)S(1)}, u32[]{:S(2)}, u32[]{:S(2)}) collective-permute-start(bf16[384,1536]{1,0:T(8,128)(2,1)S(1)} %convolution_convert_fusion), channel_id=1, source_target_pairs={{0,3},{1,2},{2,1},{3,0},{4,7},{5,6},{6,5},{7,4},{8,11},{9,10},{10,... | collective-permute-start | bytes 3538952 | tf_op jit(solution)/shard_map/ppermute | solution.py:45
  124.8 15.2 %collective-permute-start.23 = (bf16[2,24,1536]{2,1,0:T(8,128)(2,1)S(1)}, bf16[2,24,1536]{2,1,0:T(8,128)(2,1)S(1)}, u32[]{:S(2)}, u32[]{:S(2)}) collective-permute-start(bf16[2,24,1536]{2,1,0:T(8,128)(2,1)S(1)} %get-tuple-element.87), channel_id=1, source_target_pairs={{0,16},{1,17},{2,18},{3,19},{4,20},{5,21},{6,22},{7,23},{8,24},{9,... | collective-permute-start | bytes 442376 | tf_op jit(solution)/shard_map/ppermute | solution.py:35
  124.8 15.1 %collective-permute-start.27 = (bf16[2,24,1536]{2,1,0:T(8,128)(2,1)S(1)}, bf16[2,24,1536]{2,1,0:T(8,128)(2,1)S(1)}, u32[]{:S(2)}, u32[]{:S(2)}) collective-permute-start(bf16[2,24,1536]{2,1,0:T(8,128)(2,1)S(1)} %get-tuple-element.88), channel_id=1, source_target_pairs={{0,48},{1,49},{2,50},{3,51},{4,52},{5,53},{6,54},{7,55},{8,56},{9,... | collective-permute-start | bytes 442376 | tf_op jit(solution)/shard_map/ppermute | solution.py:35
  126.9 13.1 %collective-permute-start.26 = (bf16[2,24,1536]{2,1,0:T(8,128)(2,1)S(1)}, bf16[2,24,1536]{2,1,0:T(8,128)(2,1)S(1)}, u32[]{:S(2)}, u32[]{:S(2)}) collective-permute-start(bf16[2,24,1536]{2,1,0:T(8,128)(2,1)S(1)} %get-tuple-element.89), channel_id=1, source_target_pairs={{0,32},{1,33},{2,34},{3,35},{4,36},{5,37},{6,38},{7,39},{8,40},{9,... | collective-permute-start | bytes 442376 | tf_op jit(solution)/shard_map/ppermute | solution.py:35
where the time goes:
time: 141 us
  waiting for transfers between devices  54.1 us (38%)
  starting transfers between devices  47.4 us (34%)
  matrix products  19.1 us (14%)
  local copies, waits for them, and re-layouts  9.56 us (7%)
  other arithmetic  9.21 us (7%)
    ppermute x22, waiting for transfers between devices, send(): return lax.ppermute(array, AXES, pairs)  40.9 us
    ppermute x22, starting transfers between devices, send(): return lax.ppermute(array, AXES, pairs)  38 us
    dot_general x24, matrix products, dot(): lax.dot_general(left, right, ((dims[:1], dims[1:]), ((), ())), preferred_...  19.1 us
    ppermute x6, waiting for transfers between devices, exchange(): return lax.ppermute(array, AXES, pairs)  13.2 us
    ppermute x6, starting transfers between devices, exchange(): return lax.ppermute(array, AXES, pairs)  9.43 us
    dynamic_slice x1, local copies, waits for them, and re-layouts, local(): lax.dynamic_slice_in_dim(w_in, (1 - core) * 768, 768, axis=1)  4.23 us
  transfers between devices with their start and end apart: 28, of which 14 were waited for; matrix products, arithmetic and copies ran while one was open for 24% of the time, Pallas kernels for 0%

commit v1 on v0

--- a/solution.py
+++ b/solution.py
@@ -103,7 +103,7 @@
     block1, block3 = after(block1, payload1), after(block3, payload1)
     block2 = jnp.stack([send(block1[0], x=-1), send(block3[1], x=1)])
     total2 = front(block2[0], block2[1], weights)
-    payload2, arrived2 = cross(total2)
+    payload2 = total2.astype(BF)
 
     def split(rows, shift):
         def quarter(q):
@@ -126,6 +126,7 @@
     mine0 = middle(total0, after(arrived0, payload2))
     other0 = send(mine0, core=1)
     pair0 = pair_rows(mine0, other0)
+    arrived2 = send(after(payload2, other0), hi=1)
     far1 = exchange(jnp.concatenate([block2[1], token1[2], pair0[3]], axis=1), 0)
 
     mine1 = middle(total1, after(arrived1, far0))
@@ -171,11 +172,11 @@
     total = after(total, out_sent, in_sent)
     arrived = [send(total[:, 24 * k : 24 * k + 24].astype(BF), lo=k) for k in (1, 2, 3)]
 
-    sums = total[:, :24]
+    layer_sum, token_sum = total[0, :24], total[1, :24]
     for part in arrived:
-        sums = sums + after(part, grad_w_out, grad_w_in).astype(F32)
-    layer_out = sums[0].astype(BF)
-    grad_tokens = sums[1].astype(BF)
+        part = after(part, grad_w_out, grad_w_in).astype(F32)
+        layer_sum, token_sum = layer_sum + part[0], token_sum + part[1]
+    layer_out, grad_tokens = layer_sum.astype(BF), token_sum.astype(BF)
     return (layer_out, grad_tokens, grad_w_in, grad_w_out)
 
 

time: 141 us -> 141 us (level)
  transfers between devices with their start and end apart: 28 -> 28, of which waited for: 14 -> 15; matrix products, arithmetic and copies ran while one was open for 24% -> 24% of each run, Pallas kernels for 0% -> 0%
where the time goes in v1:
time: 141 us
  waiting for transfers between devices  54.1 us (38%)
  starting transfers between devices  47.4 us (34%)
  matrix products  19.1 us (14%)
  other arithmetic  9.97 us (7%)
  local copies, waits for them, and re-layouts  8.89 us (6%)
    ppermute x22, waiting for transfers between devices, send(): return lax.ppermute(array, AXES, pairs)  41 us
    ppermute x22, starting transfers between devices, send(): return lax.ppermute(array, AXES, pairs)  38 us
    dot_general x24, matrix products, dot(): lax.dot_general(left, right, ((dims[:1], dims[1:]), ((), ())), preferred_...  19.1 us
    ppermute x6, waiting for transfers between devices, exchange(): return lax.ppermute(array, AXES, pairs)  13.1 us
    ppermute x6, starting transfers between devices, exchange(): return lax.ppermute(array, AXES, pairs)  9.42 us
    dynamic_slice x1, local copies, waits for them, and re-layouts, local(): lax.dynamic_slice_in_dim(w_in, (1 - core) * 768, 768, axis=1)  4.23 us
  transfers between devices with their start and end apart: 28, of which 15 were waited for; matrix products, arithmetic and copies ran while one was open for 24% of the time, Pallas kernels for 0%

profile of v1, /device:TPU:32, one launch (start us, length us, event | category | flops | bytes accessed | tf_op | source)
XLA Modules:
  0.0 140.7 jit_solution(3061514301929756071)
XLA Ops:
  0.6 1.7 %pad_maximum_fusion.14 = bf16[2,24,1536]{2,1,0:T(8,128)(2,1)} fusion(bf16[1,24,1536]{2,1,0:T(8,128)(2,1)} %bitcast.179, bf16[1,24,1536]{2,1,0:T(8,128)(2,1)} %bitcast.181), kind=kLoop, calls=%fused_computation.197 | loop fusion | flops 73728 | bytes 294912 | tf_op jit(solution)/shard_map/stack | solution.py:94
  2.3 1.9 %collective-permute-start.2 = (bf16[2,24,1536]{2,1,0:T(8,128)(2,1)}, bf16[2,24,1536]{2,1,0:T(8,128)(2,1)S(1)}, u32[]{:S(2)}, u32[]{:S(2)}) collective-permute-start(bf16[2,24,1536]{2,1,0:T(8,128)(2,1)} %pad_maximum_fusion.14), channel_id=1, source_target_pairs={{0,16},{1,17},{2,18},{3,19},{4,20},{5,21},{6,22},{7,23},{8,24},{9,... | collective-permute-start | bytes 442376 | tf_op jit(solution)/shard_map/ppermute | solution.py:35
  4.2 2.3 %collective-permute-start.1 = (bf16[2,24,1536]{2,1,0:T(8,128)(2,1)}, bf16[2,24,1536]{2,1,0:T(8,128)(2,1)S(1)}, u32[]{:S(2)}, u32[]{:S(2)}) collective-permute-start(bf16[2,24,1536]{2,1,0:T(8,128)(2,1)} %pad_maximum_fusion.14), channel_id=1, source_target_pairs={{0,32},{1,33},{2,34},{3,35},{4,36},{5,37},{6,38},{7,39},{8,40},{9,... | collective-permute-start | bytes 442376 | tf_op jit(solution)/shard_map/ppermute | solution.py:35
  6.5 1.1 collective-permute-start
  7.6 4.2 %constant_dynamic-slice_fusion.4 = (bf16[1536,768]{1,0:T(8,128)(2,1)S(1)}, bf16[1536,768]{1,0:T(8,128)(2,1)}) fusion(bf16[1536,1536]{1,0:T(8,128)(2,1)} %param.5, s32[]{:T(128)S(6)} %select_n.141, s32[]{:T(128)S(6)} %select_n.140), kind=kLoop, calls=%fused_computation.245 | loop fusion | bytes 9437192 | tf_op jit(solution)/shard_map/dynamic_slice | solution.py:86
  11.9 2.5 %constant_dynamic-slice_fusion.2 = (bf16[768,1536]{1,0:T(8,128)(2,1)}, bf16[768,1536]{1,0:T(8,128)(2,1)}) fusion(bf16[1536,1536]{1,0:T(8,128)(2,1)S(1)} %bitcast.178, s32[]{:T(128)S(6)} %select_n.141, s32[]{:T(128)S(6)} %select_n.140), kind=kLoop, calls=%fused_computation.243 | loop fusion | bytes 9437192 | tf_op jit(solution)/shard_map/dynamic_slice | solution.py:88
  15.1 2.0 %collective-permute-done.1 = bf16[2,24,1536]{2,1,0:T(8,128)(2,1)S(1)} collective-permute-done((bf16[2,24,1536]{2,1,0:T(8,128)(2,1)}, bf16[2,24,1536]{2,1,0:T(8,128)(2,1)S(1)}, u32[]{:S(2)}, u32[]{:S(2)}) %collective-permute-start.1) | collective-permute-done | bytes 147488 | tf_op jit(solution)/shard_map/ppermute | solution.py:35
  17.1 2.0 %collective-permute-done = bf16[2,24,1536]{2,1,0:T(8,128)(2,1)S(1)} collective-permute-done((bf16[2,24,1536]{2,1,0:T(8,128)(2,1)}, bf16[2,24,1536]{2,1,0:T(8,128)(2,1)S(1)}, u32[]{:S(2)}, u32[]{:S(2)}) %collective-permute-start) | collective-permute-done | bytes 147488 | tf_op jit(solution)/shard_map/ppermute | solution.py:35
  19.2 1.6 %collective-permute-start.6 = (bf16[2,96,1536]{2,1,0:T(8,128)(2,1)S(1)}, bf16[2,96,1536]{2,1,0:T(8,128)(2,1)S(1)}, u32[]{:S(2)}, u32[]{:S(2)}) collective-permute-start(bf16[2,96,1536]{2,1,0:T(8,128)(2,1)S(1)} %pad_maximum_fusion.3), channel_id=1, source_target_pairs={{0,4},{1,5},{2,6},{3,7},{4,8},{5,9},{6,10},{7,11},{8,12},{9,13},{1... | collective-permute-start | bytes 1769480 | tf_op jit(solution)/shard_map/ppermute | solution.py:35
  20.8 1.7 %collective-permute-start.5 = (bf16[2,96,1536]{2,1,0:T(8,128)(2,1)S(1)}, bf16[2,96,1536]{2,1,0:T(8,128)(2,1)S(1)}, u32[]{:S(2)}, u32[]{:S(2)}) collective-permute-start(bf16[2,96,1536]{2,1,0:T(8,128)(2,1)S(1)} %pad_maximum_fusion.3), channel_id=1, source_target_pairs={{0,12},{1,13},{2,14},{3,15},{4,0},{5,1},{6,2},{7,3},{8,4},{9,5},{1... | collective-permute-start | bytes 1769480 | tf_op jit(solution)/shard_map/ppermute | solution.py:35
  25.8 0.8 convolution_bitcast_fusion.4
  26.7 6.1 %collective-permute-start.4 = (bf16[2,96,768]{2,1,0:T(8,128)(2,1)S(1)}, bf16[2,96,768]{2,1,0:T(8,128)(2,1)S(1)}, u32[]{:S(2)}, u32[]{:S(2)}) collective-permute-start(bf16[2,96,768]{2,1,0:T(8,128)(2,1)S(1)} %fusion.39), channel_id=1, source_target_pairs={{0,128},{1,129},{2,130},{3,131},{4,132},{5,133},{6,134},{7,135},{8... | collective-permute-start | bytes 884744 | tf_op jit(solution)/shard_map/ppermute | solution.py:35
  32.8 3.0 %collective-permute-done.5 = bf16[2,96,1536]{2,1,0:T(8,128)(2,1)S(1)} collective-permute-done((bf16[2,96,1536]{2,1,0:T(8,128)(2,1)S(1)}, bf16[2,96,1536]{2,1,0:T(8,128)(2,1)S(1)}, u32[]{:S(2)}, u32[]{:S(2)}) %collective-permute-start.5) | collective-permute-done | bytes 589856 | tf_op jit(solution)/shard_map/ppermute | solution.py:35
  36.6 0.9 fusion.12
  38.1 0.9 convolution_bitcast_fusion
  39.4 1.8 %collective-permute-done.7 = bf16[2,192,768]{2,1,0:T(8,128)(2,1)S(1)} collective-permute-done((bf16[2,192,768]{2,1,0:T(8,128)(2,1)S(1)}, bf16[2,192,768]{2,1,0:T(8,128)(2,1)S(1)}, u32[]{:S(2)}, u32[]{:S(2)}) %collective-permute-start.7) | collective-permute-done | bytes 589856 | tf_op jit(solution)/shard_map/ppermute | solution.py:35
  41.4 3.0 %collective-permute-start.8 = (bf16[96,1536]{1,0:T(8,128)(2,1)S(1)}, bf16[96,1536]{1,0:T(8,128)(2,1)S(1)}, u32[]{:S(2)}, u32[]{:S(2)}) collective-permute-start(bf16[96,1536]{1,0:T(8,128)(2,1)S(1)} %slice_bitcast_fusion.11), channel_id=1, source_target_pairs={{0,12},{1,13},{2,14},{3,15},{4,0},{5,1},{6,2},{7,3},{8,4},{9,5},{1... | collective-permute-start | bytes 884744 | tf_op jit(solution)/shard_map/ppermute | solution.py:35
  44.5 6.1 %collective-permute-start.11 = (bf16[2,192,768]{2,1,0:T(8,128)(2,1)S(1)}, bf16[2,192,768]{2,1,0:T(8,128)(2,1)S(1)}, u32[]{:S(2)}, u32[]{:S(2)}) collective-permute-start(bf16[2,192,768]{2,1,0:T(8,128)(2,1)S(1)} %fusion.17), channel_id=1, source_target_pairs={{0,128},{1,129},{2,130},{3,131},{4,132},{5,133},{6,134},{7,135},{8... | collective-permute-start | bytes 1769480 | tf_op jit(solution)/shard_map/ppermute | solution.py:35
  50.6 1.6 %collective-permute-start.12 = (bf16[288,2304]{1,0:T(8,128)(2,1)S(1)}, bf16[288,2304]{1,0:T(8,128)(2,1)S(1)}, u32[]{:S(2)}, u32[]{:S(2)}) collective-permute-start(bf16[288,2304]{1,0:T(8,128)(2,1)S(1)} %pad_maximum_fusion.1), channel_id=1, source_target_pairs={{0,1},{1,0},{2,3},{3,2},{4,5},{5,4},{6,7},{7,6},{8,9},{9,8},{10,11... | collective-permute-start | bytes 3981320 | tf_op jit(solution)/shard_map/ppermute | solution.py:45
  52.7 1.7 %collective-permute-done.9 = bf16[96,1536]{1,0:T(8,128)(2,1)S(1)} collective-permute-done((bf16[96,1536]{1,0:T(8,128)(2,1)S(1)}, bf16[96,1536]{1,0:T(8,128)(2,1)S(1)}, u32[]{:S(2)}, u32[]{:S(2)}) %collective-permute-start.9) | collective-permute-done | bytes 294944 | tf_op jit(solution)/shard_map/ppermute | solution.py:35
  54.4 0.8 fusion.16
  58.0 1.1 collective-permute-done.14
  59.0 5.8 %collective-permute-start.17 = (bf16[2,96,768]{2,1,0:T(8,128)(2,1)S(1)}, bf16[2,96,768]{2,1,0:T(8,128)(2,1)S(1)}, u32[]{:S(2)}, u32[]{:S(2)}) collective-permute-start(bf16[2,96,768]{2,1,0:T(8,128)(2,1)S(1)} %fusion.38), channel_id=1, source_target_pairs={{0,128},{1,129},{2,130},{3,131},{4,132},{5,133},{6,134},{7,135},{8... | collective-permute-start | bytes 884744 | tf_op jit(solution)/shard_map/ppermute | solution.py:35
  65.4 1.7 %collective-permute-start.18 = (bf16[96,4608]{1,0:T(8,128)(2,1)S(1)}, bf16[96,4608]{1,0:T(8,128)(2,1)S(1)}, u32[]{:S(2)}, u32[]{:S(2)}) collective-permute-start(bf16[96,4608]{1,0:T(8,128)(2,1)S(1)} %get-tuple-element.58), channel_id=1, source_target_pairs={{0,1},{1,0},{2,3},{3,2},{4,5},{5,4},{6,7},{7,6},{8,9},{9,8},{10,11... | collective-permute-start | bytes 2654216 | tf_op jit(solution)/shard_map/ppermute | solution.py:45
  67.1 15.6 %collective-permute-done.11 = bf16[2,192,768]{2,1,0:T(8,128)(2,1)S(1)} collective-permute-done((bf16[2,192,768]{2,1,0:T(8,128)(2,1)S(1)}, bf16[2,192,768]{2,1,0:T(8,128)(2,1)S(1)}, u32[]{:S(2)}, u32[]{:S(2)}) %collective-permute-start.11) | collective-permute-done | bytes 589856 | tf_op jit(solution)/shard_map/ppermute | solution.py:35
  83.8 1.8 %collective-permute-done.13 = bf16[2,192,768]{2,1,0:T(8,128)(2,1)S(1)} collective-permute-done((bf16[2,192,768]{2,1,0:T(8,128)(2,1)S(1)}, bf16[2,192,768]{2,1,0:T(8,128)(2,1)S(1)}, u32[]{:S(2)}, u32[]{:S(2)}) %collective-permute-start.13) | collective-permute-done | bytes 589856 | tf_op jit(solution)/shard_map/ppermute | solution.py:35
  86.4 1.7 %collective-permute-start.21 = (bf16[192,2304]{1,0:T(8,128)(2,1)S(1)}, bf16[192,2304]{1,0:T(8,128)(2,1)S(1)}, u32[]{:S(2)}, u32[]{:S(2)}) collective-permute-start(bf16[192,2304]{1,0:T(8,128)(2,1)S(1)} %pad_maximum_fusion.2), channel_id=1, source_target_pairs={{0,1},{1,0},{2,3},{3,2},{4,5},{5,4},{6,7},{7,6},{8,9},{9,8},{10,11... | collective-permute-start | bytes 2654216 | tf_op jit(solution)/shard_map/ppermute | solution.py:45
  89.9 0.9 fusion.32
  90.7 0.8 fusion.34
  91.7 0.9 fusion.2
  92.6 0.8 fusion.1
  94.5 2.9 %collective-permute-start.16 = (bf16[2,96,1536]{2,1,0:T(8,128)(2,1)S(1)}, bf16[2,96,1536]{2,1,0:T(8,128)(2,1)S(1)}, u32[]{:S(2)}, u32[]{:S(2)}) collective-permute-start(bf16[2,96,1536]{2,1,0:T(8,128)(2,1)S(1)} %get-tuple-element.72), channel_id=1, source_target_pairs={{0,12},{1,13},{2,14},{3,15},{4,0},{5,1},{6,2},{7,3},{8,4},{9,5},{1... | collective-permute-start | bytes 1769480 | tf_op jit(solution)/shard_map/ppermute | solution.py:35
  97.7 1.1 collective-permute-start.22
  100.2 0.8 fusion.5
  101.6 1.2 collective-permute-start.20
  103.3 2.8 %collective-permute-done.22 = bf16[96,2304]{1,0:T(8,128)(2,1)S(1)} collective-permute-done((bf16[96,2304]{1,0:T(8,128)(2,1)S(1)}, bf16[96,2304]{1,0:T(8,128)(2,1)S(1)}, u32[]{:S(2)}, u32[]{:S(2)}) %collective-permute-start.22) | collective-permute-done | bytes 442400 | tf_op jit(solution)/shard_map/ppermute | solution.py:45
  106.2 1.1 convolution_convert_fusion.1
  107.3 1.1 fusion.101
  108.4 2.6 %collective-permute-start.24 = (bf16[384,1536]{1,0:T(8,128)(2,1)S(1)}, bf16[384,1536]{1,0:T(8,128)(2,1)S(1)}, u32[]{:S(2)}, u32[]{:S(2)}) collective-permute-start(bf16[384,1536]{1,0:T(8,128)(2,1)S(1)} %convolution_convert_fusion.1), channel_id=1, source_target_pairs={{0,3},{1,2},{2,1},{3,0},{4,7},{5,6},{6,5},{7,4},{8,11},{9,10},{10,... | collective-permute-start | bytes 3538952 | tf_op jit(solution)/shard_map/ppermute | solution.py:45
  110.9 1.1 fusion.102
  112.0 1.1 convolution_convert_fusion
  113.2 0.9 collective-permute-start.25
  114.0 8.5 %collective-permute-done.16 = bf16[2,96,1536]{2,1,0:T(8,128)(2,1)S(1)} collective-permute-done((bf16[2,96,1536]{2,1,0:T(8,128)(2,1)S(1)}, bf16[2,96,1536]{2,1,0:T(8,128)(2,1)S(1)}, u32[]{:S(2)}, u32[]{:S(2)}) %collective-permute-start.16) | collective-permute-done | bytes 589856 | tf_op jit(solution)/shard_map/ppermute | solution.py:35
  122.6 1.8 %collective-permute-done.20 = bf16[2,96,1536]{2,1,0:T(8,128)(2,1)S(1)} collective-permute-done((bf16[2,96,1536]{2,1,0:T(8,128)(2,1)S(1)}, bf16[2,96,1536]{2,1,0:T(8,128)(2,1)S(1)}, u32[]{:S(2)}, u32[]{:S(2)}) %collective-permute-start.20) | collective-permute-done | bytes 589856 | tf_op jit(solution)/shard_map/ppermute | solution.py:35
  124.8 2.0 %collective-permute-start.27 = (bf16[2,24,1536]{2,1,0:T(8,128)(2,1)S(1)}, bf16[2,24,1536]{2,1,0:T(8,128)(2,1)S(1)}, u32[]{:S(2)}, u32[]{:S(2)}) collective-permute-start(bf16[2,24,1536]{2,1,0:T(8,128)(2,1)S(1)} %get-tuple-element.92), channel_id=1, source_target_pairs={{0,48},{1,49},{2,50},{3,51},{4,52},{5,53},{6,54},{7,55},{8,56},{9,... | collective-permute-start | bytes 442376 | tf_op jit(solution)/shard_map/ppermute | solution.py:35
  126.9 1.4 %add_convert_fusion.1 = bf16[384,1536]{1,0:T(8,128)(2,1)} fusion(f32[384,1536]{1,0:T(8,128)S(1)} %fusion.101, bf16[384,1536]{1,0:T(8,128)(2,1)S(1)} %collective-permute-done.24), kind=kLoop, calls=%fused_computation.13 | loop fusion | flops 1769472 | bytes 4718592 | tf_op jit(solution)/shard_map/convert_element_type | solution.py:165
  128.3 10.2 %collective-permute-done.25 = bf16[384,1536]{1,0:T(8,128)(2,1)S(1)} collective-permute-done((bf16[384,1536]{1,0:T(8,128)(2,1)S(1)}, bf16[384,1536]{1,0:T(8,128)(2,1)S(1)}, u32[]{:S(2)}, u32[]{:S(2)}) %collective-permute-start.25) | collective-permute-done | bytes 1179680 | tf_op jit(solution)/shard_map/ppermute | solution.py:45
  138.5 1.4 add_convert_fusion
  (123 shorter events, 18.4 us)
Async XLA Ops:
  0.6 11.2 %slice-start = ((s8[4718592]{0:T(1024)(128)(4,1)}), s8[524288]{0:T(1024)(128)(4,1)S(1)}, s32[]{:S(2)}) async-start(s8[4718592]{0:T(1024)(128)(4,1)} %bitcast.177), calls=%async_computation | async-start | bytes 1048576
  2.3 12.8 %collective-permute-start.2 = (bf16[2,24,1536]{2,1,0:T(8,128)(2,1)}, bf16[2,24,1536]{2,1,0:T(8,128)(2,1)S(1)}, u32[]{:S(2)}, u32[]{:S(2)}) collective-permute-start(bf16[2,24,1536]{2,1,0:T(8,128)(2,1)} %pad_maximum_fusion.14), channel_id=1, source_target_pairs={{0,16},{1,17},{2,18},{3,19},{4,20},{5,21},{6,22},{7,23},{8,24},{9,... | collective-permute-start | bytes 442376 | tf_op jit(solution)/shard_map/ppermute | solution.py:35
  4.2 12.9 %collective-permute-start.1 = (bf16[2,24,1536]{2,1,0:T(8,128)(2,1)}, bf16[2,24,1536]{2,1,0:T(8,128)(2,1)S(1)}, u32[]{:S(2)}, u32[]{:S(2)}) collective-permute-start(bf16[2,24,1536]{2,1,0:T(8,128)(2,1)} %pad_maximum_fusion.14), channel_id=1, source_target_pairs={{0,32},{1,33},{2,34},{3,35},{4,36},{5,37},{6,38},{7,39},{8,40},{9,... | collective-permute-start | bytes 442376 | tf_op jit(solution)/shard_map/ppermute | solution.py:35
  6.5 12.6 %collective-permute-start = (bf16[2,24,1536]{2,1,0:T(8,128)(2,1)}, bf16[2,24,1536]{2,1,0:T(8,128)(2,1)S(1)}, u32[]{:S(2)}, u32[]{:S(2)}) collective-permute-start(bf16[2,24,1536]{2,1,0:T(8,128)(2,1)} %pad_maximum_fusion.14), channel_id=1, source_target_pairs={{0,48},{1,49},{2,50},{3,51},{4,52},{5,53},{6,54},{7,55},{8,56},{9,... | collective-permute-start | bytes 442376 | tf_op jit(solution)/shard_map/ppermute | solution.py:35
  7.6 4.2 %slice-start.1 = ((s8[4718592]{0:T(1024)(128)(4,1)}), s8[4194304]{0:T(1024)(128)(4,1)S(1)}, s32[]{:S(2)}) async-start(s8[4718592]{0:T(1024)(128)(4,1)} %bitcast.177), calls=%async_computation.1 | async-start | bytes 8388608
  11.8 7.3 %copy-start.3 = (bf16[24,1536]{1,0:T(8,128)(2,1)S(1)}, bf16[24,1536]{1,0:T(8,128)(2,1)}, u32[]{:S(2)}) copy-start(bf16[24,1536]{1,0:T(8,128)(2,1)} %param.7) | copy-start | bytes 221188
  11.8 7.3 %copy-start.4 = (bf16[24,1536]{1,0:T(8,128)(2,1)S(1)}, bf16[24,1536]{1,0:T(8,128)(2,1)}, u32[]{:S(2)}) copy-start(bf16[24,1536]{1,0:T(8,128)(2,1)} %param.4) | copy-start | bytes 221188
  19.2 3.9 %copy-start = (bf16[768,1536]{1,0:T(8,128)(2,1)S(1)}, bf16[768,1536]{1,0:T(8,128)(2,1)}, u32[]{:S(2)}) copy-start(bf16[768,1536]{1,0:T(8,128)(2,1)} %get-tuple-element.34) | copy-start | bytes 7077892
  19.2 16.6 %collective-permute-start.6 = (bf16[2,96,1536]{2,1,0:T(8,128)(2,1)S(1)}, bf16[2,96,1536]{2,1,0:T(8,128)(2,1)S(1)}, u32[]{:S(2)}, u32[]{:S(2)}) collective-permute-start(bf16[2,96,1536]{2,1,0:T(8,128)(2,1)S(1)} %pad_maximum_fusion.3), channel_id=1, source_target_pairs={{0,4},{1,5},{2,6},{3,7},{4,8},{5,9},{6,10},{7,11},{8,12},{9,13},{1... | collective-permute-start | bytes 1769480 | tf_op jit(solution)/shard_map/ppermute | solution.py:35
  20.8 15.0 %collective-permute-start.5 = (bf16[2,96,1536]{2,1,0:T(8,128)(2,1)S(1)}, bf16[2,96,1536]{2,1,0:T(8,128)(2,1)S(1)}, u32[]{:S(2)}, u32[]{:S(2)}) collective-permute-start(bf16[2,96,1536]{2,1,0:T(8,128)(2,1)S(1)} %pad_maximum_fusion.3), channel_id=1, source_target_pairs={{0,12},{1,13},{2,14},{3,15},{4,0},{5,1},{6,2},{7,3},{8,4},{9,5},{1... | collective-permute-start | bytes 1769480 | tf_op jit(solution)/shard_map/ppermute | solution.py:35
  23.1 1.7 %copy-start.2 = (bf16[1536,768]{1,0:T(8,128)(2,1)S(1)}, bf16[1536,768]{1,0:T(8,128)(2,1)}, u32[]{:S(2)}) copy-start(bf16[1536,768]{1,0:T(8,128)(2,1)} %get-tuple-element.31) | copy-start | bytes 7077892
  23.9 1.9 %copy-start.1 = (bf16[768,1536]{1,0:T(8,128)(2,1)S(1)}, bf16[768,1536]{1,0:T(8,128)(2,1)}, u32[]{:S(2)}) copy-start(bf16[768,1536]{1,0:T(8,128)(2,1)} %get-tuple-element.32) | copy-start | bytes 7077892
  24.0 2.6 %collective-permute-start.3 = (bf16[2,96,768]{2,1,0:T(8,128)(2,1)S(1)}, bf16[2,96,768]{2,1,0:T(8,128)(2,1)S(1)}, u32[]{:S(2)}, u32[]{:S(2)}) collective-permute-start(bf16[2,96,768]{2,1,0:T(8,128)(2,1)S(1)} %pad_maximum_fusion.10), channel_id=1, source_target_pairs={{0,64},{1,65},{2,66},{3,67},{4,68},{5,69},{6,70},{7,71},{8,72},{9,... | collective-permute-start | bytes 884744 | tf_op jit(solution)/shard_map/ppermute | solution.py:35
  26.7 30.3 %collective-permute-start.4 = (bf16[2,96,768]{2,1,0:T(8,128)(2,1)S(1)}, bf16[2,96,768]{2,1,0:T(8,128)(2,1)S(1)}, u32[]{:S(2)}, u32[]{:S(2)}) collective-permute-start(bf16[2,96,768]{2,1,0:T(8,128)(2,1)S(1)} %fusion.39), channel_id=1, source_target_pairs={{0,128},{1,129},{2,130},{3,131},{4,132},{5,133},{6,134},{7,135},{8... | collective-permute-start | bytes 884744 | tf_op jit(solution)/shard_map/ppermute | solution.py:35
  39.1 2.1 %collective-permute-start.7 = (bf16[2,192,768]{2,1,0:T(8,128)(2,1)S(1)}, bf16[2,192,768]{2,1,0:T(8,128)(2,1)S(1)}, u32[]{:S(2)}, u32[]{:S(2)}) collective-permute-start(bf16[2,192,768]{2,1,0:T(8,128)(2,1)S(1)} %pad_maximum_fusion.4), channel_id=1, source_target_pairs={{0,64},{1,65},{2,66},{3,67},{4,68},{5,69},{6,70},{7,71},{8,72},{9,... | collective-permute-start | bytes 1769480 | tf_op jit(solution)/shard_map/ppermute | solution.py:35
  41.4 10.8 %collective-permute-start.8 = (bf16[96,1536]{1,0:T(8,128)(2,1)S(1)}, bf16[96,1536]{1,0:T(8,128)(2,1)S(1)}, u32[]{:S(2)}, u32[]{:S(2)}) collective-permute-start(bf16[96,1536]{1,0:T(8,128)(2,1)S(1)} %slice_bitcast_fusion.11), channel_id=1, source_target_pairs={{0,12},{1,13},{2,14},{3,15},{4,0},{5,1},{6,2},{7,3},{8,4},{9,5},{1... | collective-permute-start | bytes 884744 | tf_op jit(solution)/shard_map/ppermute | solution.py:35
  44.4 10.0 %collective-permute-start.9 = (bf16[96,1536]{1,0:T(8,128)(2,1)S(1)}, bf16[96,1536]{1,0:T(8,128)(2,1)S(1)}, u32[]{:S(2)}, u32[]{:S(2)}) collective-permute-start(bf16[96,1536]{1,0:T(8,128)(2,1)S(1)} %slice_bitcast_fusion.10), channel_id=1, source_target_pairs={{0,4},{1,5},{2,6},{3,7},{4,8},{5,9},{6,10},{7,11},{8,12},{9,13},{1... | collective-permute-start | bytes 884744 | tf_op jit(solution)/shard_map/ppermute | solution.py:35
  44.5 38.1 %collective-permute-start.11 = (bf16[2,192,768]{2,1,0:T(8,128)(2,1)S(1)}, bf16[2,192,768]{2,1,0:T(8,128)(2,1)S(1)}, u32[]{:S(2)}, u32[]{:S(2)}) collective-permute-start(bf16[2,192,768]{2,1,0:T(8,128)(2,1)S(1)} %fusion.17), channel_id=1, source_target_pairs={{0,128},{1,129},{2,130},{3,131},{4,132},{5,133},{6,134},{7,135},{8... | collective-permute-start | bytes 1769480 | tf_op jit(solution)/shard_map/ppermute | solution.py:35
  50.6 32.0 %collective-permute-start.12 = (bf16[288,2304]{1,0:T(8,128)(2,1)S(1)}, bf16[288,2304]{1,0:T(8,128)(2,1)S(1)}, u32[]{:S(2)}, u32[]{:S(2)}) collective-permute-start(bf16[288,2304]{1,0:T(8,128)(2,1)S(1)} %pad_maximum_fusion.1), channel_id=1, source_target_pairs={{0,1},{1,0},{2,3},{3,2},{4,5},{5,4},{6,7},{7,6},{8,9},{9,8},{10,11... | collective-permute-start | bytes 3981320 | tf_op jit(solution)/shard_map/ppermute | solution.py:45
  55.3 1.7 %collective-permute-start.10 = (bf16[2,96,768]{2,1,0:T(8,128)(2,1)S(1)}, bf16[2,96,768]{2,1,0:T(8,128)(2,1)S(1)}, u32[]{:S(2)}, u32[]{:S(2)}) collective-permute-start(bf16[2,96,768]{2,1,0:T(8,128)(2,1)S(1)} %pad_maximum_fusion.11), channel_id=1, source_target_pairs={{0,64},{1,65},{2,66},{3,67},{4,68},{5,69},{6,70},{7,71},{8,72},{9,... | collective-permute-start | bytes 884744 | tf_op jit(solution)/shard_map/ppermute | solution.py:35
  57.4 1.7 %collective-permute-start.14 = (bf16[2,96,768]{2,1,0:T(8,128)(2,1)S(1)}, bf16[2,96,768]{2,1,0:T(8,128)(2,1)S(1)}, u32[]{:S(2)}, u32[]{:S(2)}) collective-permute-start(bf16[2,96,768]{2,1,0:T(8,128)(2,1)S(1)} %pad_maximum_fusion.12), channel_id=1, source_target_pairs={{0,64},{1,65},{2,66},{3,67},{4,68},{5,69},{6,70},{7,71},{8,72},{9,... | collective-permute-start | bytes 884744 | tf_op jit(solution)/shard_map/ppermute | solution.py:35
  59.0 29.8 %collective-permute-start.17 = (bf16[2,96,768]{2,1,0:T(8,128)(2,1)S(1)}, bf16[2,96,768]{2,1,0:T(8,128)(2,1)S(1)}, u32[]{:S(2)}, u32[]{:S(2)}) collective-permute-start(bf16[2,96,768]{2,1,0:T(8,128)(2,1)S(1)} %fusion.38), channel_id=1, source_target_pairs={{0,128},{1,129},{2,130},{3,131},{4,132},{5,133},{6,134},{7,135},{8... | collective-permute-start | bytes 884744 | tf_op jit(solution)/shard_map/ppermute | solution.py:35
  65.4 26.2 %collective-permute-start.18 = (bf16[96,4608]{1,0:T(8,128)(2,1)S(1)}, bf16[96,4608]{1,0:T(8,128)(2,1)S(1)}, u32[]{:S(2)}, u32[]{:S(2)}) collective-permute-start(bf16[96,4608]{1,0:T(8,128)(2,1)S(1)} %get-tuple-element.58), channel_id=1, source_target_pairs={{0,1},{1,0},{2,3},{3,2},{4,5},{5,4},{6,7},{7,6},{8,9},{9,8},{10,11... | collective-permute-start | bytes 2654216 | tf_op jit(solution)/shard_map/ppermute | solution.py:45
  83.5 2.1 %collective-permute-start.13 = (bf16[2,192,768]{2,1,0:T(8,128)(2,1)S(1)}, bf16[2,192,768]{2,1,0:T(8,128)(2,1)S(1)}, u32[]{:S(2)}, u32[]{:S(2)}) collective-permute-start(bf16[2,192,768]{2,1,0:T(8,128)(2,1)S(1)} %pad_maximum_fusion.5), channel_id=1, source_target_pairs={{0,64},{1,65},{2,66},{3,67},{4,68},{5,69},{6,70},{7,71},{8,72},{9,... | collective-permute-start | bytes 1769480 | tf_op jit(solution)/shard_map/ppermute | solution.py:35
  86.4 16.7 %collective-permute-start.21 = (bf16[192,2304]{1,0:T(8,128)(2,1)S(1)}, bf16[192,2304]{1,0:T(8,128)(2,1)S(1)}, u32[]{:S(2)}, u32[]{:S(2)}) collective-permute-start(bf16[192,2304]{1,0:T(8,128)(2,1)S(1)} %pad_maximum_fusion.2), channel_id=1, source_target_pairs={{0,1},{1,0},{2,3},{3,2},{4,5},{5,4},{6,7},{7,6},{8,9},{9,8},{10,11... | collective-permute-start | bytes 2654216 | tf_op jit(solution)/shard_map/ppermute | solution.py:45
  89.2 8.2 %collective-permute-start.19 = (bf16[2,96,768]{2,1,0:T(8,128)(2,1)S(1)}, bf16[2,96,768]{2,1,0:T(8,128)(2,1)S(1)}, u32[]{:S(2)}, u32[]{:S(2)}) collective-permute-start(bf16[2,96,768]{2,1,0:T(8,128)(2,1)S(1)} %pad_maximum_fusion.13), channel_id=1, source_target_pairs={{0,64},{1,65},{2,66},{3,67},{4,68},{5,69},{6,70},{7,71},{8,72},{9,... | collective-permute-start | bytes 884744 | tf_op jit(solution)/shard_map/ppermute | solution.py:35
  93.8 20.2 %collective-permute-start.15 = (bf16[2,96,1536]{2,1,0:T(8,128)(2,1)S(1)}, bf16[2,96,1536]{2,1,0:T(8,128)(2,1)S(1)}, u32[]{:S(2)}, u32[]{:S(2)}) collective-permute-start(bf16[2,96,1536]{2,1,0:T(8,128)(2,1)S(1)} %get-tuple-element.71), channel_id=1, source_target_pairs={{0,4},{1,5},{2,6},{3,7},{4,8},{5,9},{6,10},{7,11},{8,12},{9,13},{1... | collective-permute-start | bytes 1769480 | tf_op jit(solution)/shard_map/ppermute | solution.py:35
  94.5 28.1 %collective-permute-start.16 = (bf16[2,96,1536]{2,1,0:T(8,128)(2,1)S(1)}, bf16[2,96,1536]{2,1,0:T(8,128)(2,1)S(1)}, u32[]{:S(2)}, u32[]{:S(2)}) collective-permute-start(bf16[2,96,1536]{2,1,0:T(8,128)(2,1)S(1)} %get-tuple-element.72), channel_id=1, source_target_pairs={{0,12},{1,13},{2,14},{3,15},{4,0},{5,1},{6,2},{7,3},{8,4},{9,5},{1... | collective-permute-start | bytes 1769480 | tf_op jit(solution)/shard_map/ppermute | solution.py:35
  97.7 8.4 %collective-permute-start.22 = (bf16[96,2304]{1,0:T(8,128)(2,1)S(1)}, bf16[96,2304]{1,0:T(8,128)(2,1)S(1)}, u32[]{:S(2)}, u32[]{:S(2)}) collective-permute-start(bf16[96,2304]{1,0:T(8,128)(2,1)S(1)} %pad_maximum_fusion.9), channel_id=1, source_target_pairs={{0,1},{1,0},{2,3},{3,2},{4,5},{5,4},{6,7},{7,6},{8,9},{9,8},{10,11... | collective-permute-start | bytes 1327112 | tf_op jit(solution)/shard_map/ppermute | solution.py:45
  101.6 22.8 %collective-permute-start.20 = (bf16[2,96,1536]{2,1,0:T(8,128)(2,1)S(1)}, bf16[2,96,1536]{2,1,0:T(8,128)(2,1)S(1)}, u32[]{:S(2)}, u32[]{:S(2)}) collective-permute-start(bf16[2,96,1536]{2,1,0:T(8,128)(2,1)S(1)} %pad_maximum_fusion.6), channel_id=1, source_target_pairs={{0,8},{1,9},{2,10},{3,11},{4,12},{5,13},{6,14},{7,15},{8,0},{9,1},... | collective-permute-start | bytes 1769480 | tf_op jit(solution)/shard_map/ppermute | solution.py:35
  108.4 18.5 %collective-permute-start.24 = (bf16[384,1536]{1,0:T(8,128)(2,1)S(1)}, bf16[384,1536]{1,0:T(8,128)(2,1)S(1)}, u32[]{:S(2)}, u32[]{:S(2)}) collective-permute-start(bf16[384,1536]{1,0:T(8,128)(2,1)S(1)} %convolution_convert_fusion.1), channel_id=1, source_target_pairs={{0,3},{1,2},{2,1},{3,0},{4,7},{5,6},{6,5},{7,4},{8,11},{9,10},{10,... | collective-permute-start | bytes 3538952 | tf_op jit(solution)/shard_map/ppermute | solution.py:45
  113.2 25.3 %collective-permute-start.25 = (bf16[384,1536]{1,0:T(8,128)(2,1)S(1)}, bf16[384,1536]{1,0:T(8,128)(2,1)S(1)}, u32[]{:S(2)}, u32[]{:S(2)}) collective-permute-start(bf16[384,1536]{1,0:T(8,128)(2,1)S(1)} %convolution_convert_fusion), channel_id=1, source_target_pairs={{0,3},{1,2},{2,1},{3,0},{4,7},{5,6},{6,5},{7,4},{8,11},{9,10},{10,... | collective-permute-start | bytes 3538952 | tf_op jit(solution)/shard_map/ppermute | solution.py:45
  124.8 15.2 %collective-permute-start.23 = (bf16[2,24,1536]{2,1,0:T(8,128)(2,1)S(1)}, bf16[2,24,1536]{2,1,0:T(8,128)(2,1)S(1)}, u32[]{:S(2)}, u32[]{:S(2)}) collective-permute-start(bf16[2,24,1536]{2,1,0:T(8,128)(2,1)S(1)} %get-tuple-element.91), channel_id=1, source_target_pairs={{0,16},{1,17},{2,18},{3,19},{4,20},{5,21},{6,22},{7,23},{8,24},{9,... | collective-permute-start | bytes 442376 | tf_op jit(solution)/shard_map/ppermute | solution.py:35
  124.8 15.1 %collective-permute-start.27 = (bf16[2,24,1536]{2,1,0:T(8,128)(2,1)S(1)}, bf16[2,24,1536]{2,1,0:T(8,128)(2,1)S(1)}, u32[]{:S(2)}, u32[]{:S(2)}) collective-permute-start(bf16[2,24,1536]{2,1,0:T(8,128)(2,1)S(1)} %get-tuple-element.92), channel_id=1, source_target_pairs={{0,48},{1,49},{2,50},{3,51},{4,52},{5,53},{6,54},{7,55},{8,56},{9,... | collective-permute-start | bytes 442376 | tf_op jit(solution)/shard_map/ppermute | solution.py:35
  126.9 13.1 %collective-permute-start.26 = (bf16[2,24,1536]{2,1,0:T(8,128)(2,1)S(1)}, bf16[2,24,1536]{2,1,0:T(8,128)(2,1)S(1)}, u32[]{:S(2)}, u32[]{:S(2)}) collective-permute-start(bf16[2,24,1536]{2,1,0:T(8,128)(2,1)S(1)} %get-tuple-element.93), channel_id=1, source_target_pairs={{0,32},{1,33},{2,34},{3,35},{4,36},{5,37},{6,38},{7,39},{8,40},{9,... | collective-permute-start | bytes 442376 | tf_op jit(solution)/shard_map/ppermute | solution.py:35
